TPU v7x, 32 devices: a whole 2x2x4 slice. The times are simulated.
32 devices in a mesh: row: 4 (over x, core), col: 8 (over z, y).
Axes of the slice: x: 2, y: 2, z: 4, core: 2. Of those that a mesh axis runs over, the one named last changes fastest.
Arguments:
- factor_panel: bfloat16 [3584, 98304], P('row', 'col'), may hold values from -1 to 1, as said below
- normal_draws: bfloat16 [98304, 256], P('col'), may hold values from -6 to 6
- inter_event: float32 [256], replicated, may hold values from -2.5 to 2.5
- site_owner: int32 [3584], replicated, may hold values from 0 to 31, as said below
- asset_site: int32 [65536], P(('row', 'col')), may hold values from 0 to 3583, as said below
- asset_class: int32 [65536], P(('row', 'col')), may hold values from 0 to 127
- asset_value: bfloat16 [65536], P(('row', 'col')), may hold values from 0.19921875 to 5
- asset_count: int32 [32], P(('row', 'col')), may hold values from 512 to 2048, as said below
- damage_curve: bfloat16 [32, 128], replicated, may hold values from 0 to 1
Outputs:
- residuals: float32 [3584, 256], P(('row', 'col'))
- asset_loss: float32 [65536, 256], P(('row', 'col'))
- region_loss: float32 [8, 256], P('col')
Inputs may be any that keep to these rules, and one draw needn't show every extreme that they name: `factor_panel`: row i is zero beyond column 94720 + i and holds 0.7 there. `site_owner`: each aligned block of 112 sites (block d for device d = row index * 8 + col index) names each owner at most 7 times; some owner is named 7 times in every block; every owner is named somewhere. `asset_site`: every asset of block d of 2048 slots lies at a site whose owner is d. `asset_count`: some block has all 2048 slots live.
All inputs are finite; a program needn't handle non-finite values.
Results may differ from a plain program's by a relative error of at most 0.0037.
Values may be sent and summed in bfloat16 or wider, within the bound.
A program may use at most 128 MiB of HBM per device.

v0:
```python
import functools

import jax
import jax.numpy as jnp
from jax import lax
from jax.experimental import pallas as pl
from jax.experimental.pallas import tpu as pltpu
from jax.sharding import PartitionSpec as P

median_log = -1.0
intra_scale = 0.6
grid_low = -4.0
grid_span = 6.0
SLOT = 8
MESH = pl.DeviceIdType.MESH


def block_order(groups):
    order = [("A", g) for g in range(min(2, groups - 1))]
    done = 0
    for g in range(2, groups - 1):
        order += [("A", g), ("B", done)]
        done += 1
    order += [("B", g) for g in range(done, groups - 1)]
    order += [("A", groups - 1), ("B", groups - 1)]
    return order


def earlier_mask(size):
    i = lax.broadcasted_iota(jnp.int32, (size, size), 0)
    j = lax.broadcasted_iota(jnp.int32, (size, size), 1)
    return (i < j).astype(jnp.float32).astype(jnp.bfloat16)


def motion_kernel(
    rows, cols, window,
    count_ref, factor, draws, inter, owner, site_ref, class_ref, value_ref, curve_ref,
    res_ref, loss_ref, region_ref,
    fbuf, dbuf, ysend, yrecv, keep, zsend, zrecv, placing, outbuf, inbuf, select_ref, table_ref, regions,
    fsem, dsem, yssem, yrsem, zssem, zrsem, ssem, rsem, gssem, grsem,
):
    devices = rows * cols
    groups = cols // 2
    sites, depth = factor.shape[0] // cols, factor.shape[1]
    events = draws.shape[1]
    half = events // 2
    chunks = dsem.shape[0]
    cut = depth // chunks
    row, col = lax.axis_index("row"), lax.axis_index("col")
    me = row * cols + col
    side = lax.rem(col, 2)
    group = col // 2
    order = block_order(groups)
    steps = [order[i : i + 2] for i in range(0, len(order) - 2, 2)] + [[order[-2]], [order[-1]]]

    def group_at(g):
        return lax.rem(group + 1 + g, groups)

    def fetch(i):
        kind, g = order[i]
        target = group_at(g) * 2 + ((1 - side) if kind == "A" else side)
        start = pl.multiple_of(target * sites, 16)
        return pltpu.make_async_copy(
            factor.at[pl.ds(start, sites)], fbuf.at[pl.ds(i * sites, sites)], fsem.at[i]
        )

    def fetch_draws(j):
        part = pl.ds(j * cut, cut)
        return pltpu.make_async_copy(draws.at[part], dbuf.at[part], dsem.at[j])

    fetch_draws(0).start()
    for i in range(len(steps[0])):
        fetch(i).start()
    for j in range(1, chunks):
        fetch_draws(j).start()
    started = len(steps[0])
    while started < min(window, len(order)):
        fetch(started).start()
        started += 1

    barrier = pltpu.get_barrier_semaphore()

    @pl.loop(1, devices)
    def _(i):
        to = lax.rem(me + i, devices)
        pl.semaphore_signal(
            barrier, inc=1, device_id=(to // cols, lax.rem(to, cols)), device_id_type=MESH
        )

    own = owner[pl.ds(me, 1), :]
    onehot = lax.broadcasted_iota(jnp.int32, (devices, sites), 0) == own
    onehot = onehot.astype(jnp.float32)
    before = jnp.dot(
        onehot.astype(jnp.bfloat16), earlier_mask(sites), preferred_element_type=jnp.float32
    )
    rank = jnp.sum(onehot * before, axis=0, keepdims=True).astype(jnp.int32)
    slot = lax.broadcasted_iota(jnp.int32, (devices * SLOT, sites), 0)
    placing[...] = (slot == own * SLOT + rank).astype(jnp.float32).astype(jnp.bfloat16)

    prepare_assets(
        me, count_ref[0], owner, site_ref, class_ref, value_ref, curve_ref, select_ref, table_ref
    )

    def send_side(g):
        return pltpu.make_async_remote_copy(
            src_ref=ysend.at[g], dst_ref=yrecv.at[g], send_sem=yssem.at[g], recv_sem=yrsem.at[g],
            device_id=(row, col + 1 - 2 * side), device_id_type=MESH,
        )

    def send_group(g):
        return pltpu.make_async_remote_copy(
            src_ref=zsend.at[g], dst_ref=zrecv.at[g], send_sem=zssem.at[g], recv_sem=zrsem.at[g],
            device_id=(row, group_at(g) * 2 + side), device_id_type=MESH,
        )

    first = 0
    for n, step in enumerate(steps):
        count = len(step)
        for i in range(first, first + count):
            fetch(i).wait()
            if started < len(order):
                fetch(started).start()
                started += 1
        lo, hi = first * sites, (first + count) * sites
        if n == 0:
            acc = jnp.zeros((count * sites, events), jnp.float32)
            for j in range(chunks):
                fetch_draws(j).wait()
                acc += jnp.dot(
                    fbuf[lo:hi, j * cut : (j + 1) * cut], dbuf[j * cut : (j + 1) * cut, :],
                    preferred_element_type=jnp.float32,
                )
            pl.semaphore_wait(barrier, devices - 1)
        else:
            acc = jnp.dot(fbuf[lo:hi, :], dbuf[...], preferred_element_type=jnp.float32)
        for b, (kind, g) in enumerate(step):
            part = acc[b * sites : (b + 1) * sites]
            if kind == "A":
                ysend[g] = part.astype(jnp.bfloat16)
                send_side(g).start()
            else:
                send_side(g).wait_recv()
                part = part + yrecv[g].astype(jnp.float32)
                if g < groups - 1:
                    zsend[g] = part.astype(jnp.bfloat16)
                    send_group(g).start()
                else:
                    keep[...] = part
        first += count

    total = keep[...]
    for g in range(groups - 1):
        send_group(g).wait_recv()
        total = total + zrecv[g].astype(jnp.float32)
    res_ref[...] = total
    motion = (median_log + intra_scale * total + inter[...]).astype(jnp.bfloat16)
    parts = [
        jnp.dot(placing[...], motion[:, h * half : (h + 1) * half], preferred_element_type=jnp.float32)
        .reshape(devices, SLOT, half)
        for h in range(2)
    ]
    outbuf[...] = jnp.concatenate(parts, axis=1).astype(jnp.bfloat16)

    @pl.loop(1, devices)
    def _(i):
        to = lax.rem(me + i, devices)
        pltpu.make_async_remote_copy(
            src_ref=outbuf.at[to], dst_ref=inbuf.at[me], send_sem=ssem, recv_sem=rsem,
            device_id=(to // cols, lax.rem(to, cols)), device_id_type=MESH,
        ).start()

    inbuf[me] = outbuf[me]
    for g in range(groups):
        send_side(g).wait_send()
    for g in range(groups - 1):
        send_group(g).wait_send()
    others = pl.ds(0, devices - 1)
    pltpu.make_async_copy(inbuf.at[others], inbuf.at[others], rsem).wait()
    came = inbuf[...].astype(jnp.float32)
    arrived = jnp.concatenate(
        [
            came[:, h * SLOT : (h + 1) * SLOT, :].reshape(devices * SLOT, half).astype(jnp.bfloat16)
            for h in range(2)
        ],
        axis=1,
    )
    regions[0] = losses(curve_ref.shape[0], arrived, select_ref, table_ref, loss_ref)
    copies = []
    for i in range(1, rows):
        copy = pltpu.make_async_remote_copy(
            src_ref=regions.at[0], dst_ref=regions.at[i], send_sem=gssem.at[i], recv_sem=grsem.at[i],
            device_id=(lax.rem(row + i, rows), col), device_id_type=MESH,
        )
        copy.start()
        copies.append(copy)
    pltpu.make_async_copy(outbuf.at[others], outbuf.at[others], ssem).wait()
    total = regions[0]
    for i, copy in enumerate(copies):
        copy.wait_recv()
        total = total + regions[i + 1]
    scale = 1.0 / (loss_ref.shape[0] * rows)
    region_ref[...] = jnp.sum(total, axis=0, keepdims=True) * scale
    for copy in copies:
        copy.wait_send()


def prepare_assets(me, count, owner, site_ref, class_ref, value_ref, curve_ref, select_ref, table_ref):
    devices, sites = owner.shape
    slots = select_ref.shape[0]
    assets = site_ref.shape[1]
    levels, classes = curve_ref.shape
    tile = min(assets, 512)
    wide = jnp.broadcast_to(owner[...][:, None, :], (devices, SLOT, sites)).reshape(slots, sites)
    mine = (wide == me).astype(jnp.float32)
    rank = jnp.dot(mine.astype(jnp.bfloat16), earlier_mask(sites), preferred_element_type=jnp.float32)
    slot = lax.broadcasted_iota(jnp.int32, (slots, sites), 0)
    wanted = lax.rem(slot, SLOT).astype(jnp.float32)
    number = (slot // SLOT) * sites + lax.broadcasted_iota(jnp.int32, (slots, sites), 1) + 1
    hit = jnp.where((mine > 0.0) & (rank == wanted), number, 0)
    mysite = jnp.sum(hit, axis=1, keepdims=True) - 1
    curve = curve_ref[...].astype(jnp.float32)
    curve = jnp.concatenate([curve, jnp.zeros((128 - levels, classes), jnp.float32)], axis=0)
    curve = curve.astype(jnp.bfloat16)
    value = value_ref[...].astype(jnp.float32)
    for base in range(0, assets, tile):
        at = slice(base, base + tile)
        select = (mysite == site_ref[:, at]).astype(jnp.float32)
        owned = jnp.sum(select, axis=0, keepdims=True)
        select_ref[:, at] = select.astype(jnp.bfloat16)
        place = base + lax.broadcasted_iota(jnp.int32, (1, tile), 1)
        live = jnp.where(place < count, owned, 0.0)
        first = base // 128
        price = jnp.concatenate([value[first + i : first + i + 1] for i in range(tile // 128)], axis=1)
        chosen = lax.broadcasted_iota(jnp.int32, (classes, tile), 0) == class_ref[:, at]
        chosen = jnp.where(chosen, price * live, 0.0).astype(jnp.bfloat16)
        table_ref[at, :] = lax.dot_general(
            chosen, curve, (((0,), (1,)), ((), ())), preferred_element_type=jnp.float32
        )


def losses(levels, motion, select_ref, table_ref, loss_ref):
    assets, events = loss_ref.shape
    tile = min(assets, 256)
    parts = [jnp.zeros((8, 128), jnp.float32) for _ in range(events // 128)]
    for base in range(0, assets, tile):
        at = slice(base, base + tile)
        table = table_ref[at, :]
        felt = lax.dot_general(
            select_ref[:, at], motion, (((0,), (0,)), ((), ())), preferred_element_type=jnp.float32
        )
        level = jnp.clip((felt - grid_low) * ((levels - 1) / grid_span), 0.0, levels - 1.0)
        below = jnp.minimum(level.astype(jnp.int32), levels - 2)
        share = level - below.astype(jnp.float32)
        for h in range(events // 128):
            part = slice(h * 128, (h + 1) * 128)
            index = below[:, part]
            low = jnp.take_along_axis(table, index, axis=1, mode="promise_in_bounds")
            high = jnp.take_along_axis(table, index + 1, axis=1, mode="promise_in_bounds")
            loss = low + share[:, part] * (high - low)
            loss_ref[at, part] = loss
            parts[h] = parts[h] + jnp.sum(loss.reshape(tile // 8, 8, 128), axis=0)
    return jnp.concatenate(parts, axis=1)


def body(
    rows, cols,
    factor_panel, normal_draws, inter_event, site_owner, asset_site, asset_class, asset_value, asset_count, damage_curve,
):
    devices = rows * cols
    groups = cols // 2
    local, depth = factor_panel.shape
    sites = local // cols
    events = normal_draws.shape[1]
    assets = asset_site.shape[0]
    slots = devices * SLOT
    chunks = 3
    owner = site_owner.reshape(devices, sites)
    vmem = pl.BlockSpec(memory_space=pltpu.VMEM)
    hbm = pl.BlockSpec(memory_space=pl.ANY)
    dma = pltpu.SemaphoreType.DMA
    bf16, f32 = jnp.bfloat16, jnp.float32
    smem = pl.BlockSpec(memory_space=pltpu.SMEM)
    return pl.pallas_call(
        functools.partial(motion_kernel, rows, cols, max(4, cols // 2)),
        out_shape=(
            jax.ShapeDtypeStruct((sites, events), f32),
            jax.ShapeDtypeStruct((assets, events), f32),
            jax.ShapeDtypeStruct((1, events), f32),
        ),
        in_specs=[smem, hbm, hbm] + [vmem] * 6,
        out_specs=(vmem, vmem, vmem),
        scratch_shapes=[
            pltpu.VMEM((local, depth), bf16),
            pltpu.VMEM((depth, events), bf16),
            pltpu.VMEM((groups, sites, events), bf16),
            pltpu.VMEM((groups, sites, events), bf16),
            pltpu.VMEM((sites, events), f32),
            pltpu.VMEM((groups, sites, events), bf16),
            pltpu.VMEM((groups, sites, events), bf16),
            pltpu.VMEM((slots, sites), bf16),
            pltpu.VMEM((devices, 2 * SLOT, events // 2), bf16),
            pltpu.VMEM((devices, 2 * SLOT, events // 2), bf16),
            pltpu.VMEM((slots, assets), bf16),
            pltpu.VMEM((assets, 128), f32),
            pltpu.VMEM((rows, 8, events), f32),
            dma((cols,)), dma((chunks,)), dma((groups,)), dma((groups,)), dma((groups,)), dma((groups,)),
            dma, dma, dma((rows,)), dma((rows,)),
        ],
        compiler_params=pltpu.CompilerParams(
            collective_id=0, has_side_effects=True, vmem_limit_bytes=48 << 20
        ),
        name="everything",
    )(
        asset_count, factor_panel, normal_draws, inter_event.reshape(1, events), owner,
        asset_site.reshape(1, assets), asset_class.reshape(1, assets),
        asset_value.reshape(assets // 128, 128), damage_curve,
    )


def solution(mesh):
    placed = (
        P("row", "col"),
        P("col", None),
        P(),
        P(),
        P(("row", "col")),
        P(("row", "col")),
        P(("row", "col")),
        P(("row", "col")),
        P(),
    )
    return jax.shard_map(
        functools.partial(body, mesh.shape["row"], mesh.shape["col"]),
        mesh=mesh,
        in_specs=placed,
        out_specs=(P(("row", "col"), None), P(("row", "col"), None), P("col", None)),
        check_vma=False,
    )
```

profile of v0, /device:TPU:0, one launch (start us, length us, event | category | flops | bytes accessed | tf_op | source)
XLA Modules:
  0.0 43.8 jit_solution(2919781385362830315)
XLA Ops:
  1.3 0.8 %reshape.22.owner = s32[32,112]{1,0:T(8,128)S(1)} reshape(s32[3584]{0:T(1024)} %param.12) | data formatting | bytes 28672 | tf_op jit(solution)/shard_map/reshape | solution.py:277
  2.1 0.0 copy-start
  2.1 0.7 %copy-done = s32[2048]{0:T(1024)S(1)} copy-done((s32[2048]{0:T(1024)S(1)}, s32[2048]{0:T(1024)}, u32[]{:S(2)}) %copy-start) | copy-done | bytes 8216
  2.8 0.0 copy-start.1
  2.8 0.7 %copy-done.1 = s32[2048]{0:T(1024)S(1)} copy-done((s32[2048]{0:T(1024)S(1)}, s32[2048]{0:T(1024)}, u32[]{:S(2)}) %copy-start.1) | copy-done | bytes 8216
  3.5 0.0 copy-start.2
  3.5 0.7 %copy-done.2 = bf16[32,128]{1,0:T(8,128)(2,1)S(1)} copy-done((bf16[32,128]{1,0:T(8,128)(2,1)S(1)}, bf16[32,128]{1,0:T(8,128)(2,1)}, u32[]{:S(2)}) %copy-start.2) | copy-done | bytes 8216
  4.2 0.0 copy-start.3
  4.2 0.7 %copy-done.3 = bf16[2048]{0:T(1024)(128)(2,1)S(1)} copy-done((bf16[2048]{0:T(1024)(128)(2,1)S(1)}, bf16[2048]{0:T(1024)(128)(2,1)}, u32[]{:S(2)}) %copy-start.3) | copy-done | bytes 4120
  4.9 0.0 copy-start.4
  4.9 0.7 %copy-done.4 = f32[256]{0:T(256)S(1)} copy-done((f32[256]{0:T(256)S(1)}, f32[256]{0:T(256)}, u32[]{:S(2)}) %copy-start.4) | copy-done | bytes 1048
  5.5 35.8 %everything.1 = (f32[112,256]{1,0:T(8,128)S(1)}, f32[2048,256]{1,0:T(8,128)S(1)}, f32[1,256]{1,0:T(1,128)S(1)}) custom-call(s32[1]{0:T(128)S(6)} %copy.15.count_ref, bf16[896,12288]{1,0:T(8,128)(2,1)} %factor.1, bf16[12288,256]{1,0:T(8,128)(2,1)} %draws.1, f32[1,256]{1,0:T(1,128)S(1)} %bitcast.7, s32[32,112]{1,0:T(8,128)S(1)} %reshape.22.owner, ...), custom_call_target="tpu_custom_call" | custom-call | tf_op jit(solution)/shard_map/everything/pallas_call | solution.py:283
  41.3 0.6 %copy.16 = f32[112,256]{1,0:T(8,128)} copy(f32[112,256]{1,0:T(8,128)S(1)} %get-tuple-element.6) | data formatting | bytes 229376
  42.0 1.3 %copy.17 = f32[2048,256]{1,0:T(8,128)} copy(f32[2048,256]{1,0:T(8,128)S(1)} %get-tuple-element.7) | data formatting | bytes 4194304
  43.3 0.6 %copy.18 = f32[1,256]{1,0:T(1,128)} copy(f32[1,256]{1,0:T(1,128)S(1)} %get-tuple-element.8) | data formatting | bytes 2048
Async XLA Ops:
  2.1 0.7 %copy-start = (s32[2048]{0:T(1024)S(1)}, s32[2048]{0:T(1024)}, u32[]{:S(2)}) copy-start(s32[2048]{0:T(1024)} %param.13) | copy-start | bytes 24580
  2.8 0.7 %copy-start.1 = (s32[2048]{0:T(1024)S(1)}, s32[2048]{0:T(1024)}, u32[]{:S(2)}) copy-start(s32[2048]{0:T(1024)} %param.14) | copy-start | bytes 24580
  3.5 0.7 %copy-start.2 = (bf16[32,128]{1,0:T(8,128)(2,1)S(1)}, bf16[32,128]{1,0:T(8,128)(2,1)}, u32[]{:S(2)}) copy-start(bf16[32,128]{1,0:T(8,128)(2,1)} %curve_ref.1) | copy-start | bytes 24580
  4.2 0.7 %copy-start.3 = (bf16[2048]{0:T(1024)(128)(2,1)S(1)}, bf16[2048]{0:T(1024)(128)(2,1)}, u32[]{:S(2)}) copy-start(bf16[2048]{0:T(1024)(128)(2,1)} %param.15) | copy-start | bytes 12292
  4.9 0.7 %copy-start.4 = (f32[256]{0:T(256)S(1)}, f32[256]{0:T(256)}, u32[]{:S(2)}) copy-start(f32[256]{0:T(256)} %param.11) | copy-start | bytes 3076
where the time goes:
time: 44.3 us; the launch traced here: 43.8 us
  Pallas kernels  35.8 us (81%)
  local copies, waits for them, and re-layouts  6.77 us (15%)
  between operations  1.3 us (3%)
    pallas_call x1, Pallas kernels, body(): pl.pallas_call(functools.partial(motion_kernel, rows, cols, max(4, cols /...  35.8 us
    unnamed x13, local copies, waits for them, and re-layouts  5.98 us

commit v1 on v0

v1 whole, which is shorter than its diff:
```python
import functools

import jax
import jax.numpy as jnp
from jax import lax
from jax.experimental import pallas as pl
from jax.experimental.pallas import tpu as pltpu
from jax.sharding import PartitionSpec as P

median_log = -1.0
intra_scale = 0.6
grid_low = -4.0
grid_span = 6.0
SLOT = 8
TILE = 256
K1 = 60 * 1024
K2 = 60
PARTS = 8
WINDOW = 4
PAIRED = True
MESH = pl.DeviceIdType.MESH


def block_order(groups):
    ahead = min(3, groups - 1)
    order = [("A", g) for g in range(ahead)]
    order.append(("B", 0))
    for g in range(ahead, groups):
        order += [("B", g - ahead + 1), ("A", g)]
    return order + [("B", g) for g in range(groups - ahead + 1, groups)]


def earlier_mask(size):
    i = lax.broadcasted_iota(jnp.int32, (size, size), 0)
    j = lax.broadcasted_iota(jnp.int32, (size, size), 1)
    return (i < j).astype(jnp.float32).astype(jnp.bfloat16)


def motion_kernel(
    rows, cols,
    count_hbm, factor, draws, inter_hbm, owner_hbm, site_hbm, class_hbm, value_hbm, curve_hbm,
    res_out, loss_out, region_out,
    res_ref, loss_ref, region_ref, select_ref, table_ref, stage_ref, fbuf, dbuf, ysend, yrecv, held, zsend, zrecv, placing, outbuf, inbuf, regions, agg_ref, owner,
    count_ref, inter, flat, site_ref, class_ref, value_ref, curve_ref,
    fsem, dsem, yssem, yrsem, zssem, zrsem, ssem, rsem, gssem, grsem, smallsem, outsem,
):
    devices = rows * cols
    groups = cols // 2
    sites, depth = factor.shape[0] // cols, factor.shape[1]
    events = draws.shape[1]
    half = events // 2
    chunks = dsem.shape[0]
    cut = depth // chunks
    row, col = lax.axis_index("row"), lax.axis_index("col")
    me = row * cols + col
    side = lax.rem(col, 2)
    group = col // 2
    order = block_order(groups)
    width = 2 if PAIRED else 1
    steps = [order[i : i + width] for i in range(0, len(order), width)]
    sent_at = {block: n for n, step in enumerate(steps) for block in step}

    small = [
        pltpu.make_async_copy(src, dst, smallsem.at[i])
        for i, (src, dst) in enumerate(
            [
                (owner_hbm, flat), (site_hbm, site_ref), (class_hbm, class_ref), (value_hbm, value_ref),
                (curve_hbm, curve_ref), (inter_hbm, inter), (count_hbm, count_ref),
            ]
        )
    ]

    def group_at(g):
        return lax.rem(group + 1 + g, groups)

    def fetch(i):
        kind, g = order[i]
        target = group_at(g) * 2 + ((1 - side) if kind == "A" else side)
        start = pl.multiple_of(target * sites, 16)
        return pltpu.make_async_copy(
            factor.at[pl.ds(start, sites)], fbuf.at[pl.ds(i * sites, sites)], fsem.at[i]
        )

    def fetch_draws(j):
        part = pl.ds(j * cut, cut)
        return pltpu.make_async_copy(draws.at[part], dbuf.at[part], dsem.at[j])

    fetches = [functools.partial(fetch, i) for i in range(width)]
    fetches += [functools.partial(fetch_draws, j) for j in range(chunks)]
    fetches += [functools.partial(fetch, i) for i in range(width, len(order))]
    state = {"started": 0, "arrived": 0}

    def start_to(n):
        while state["started"] < min(n, len(fetches)):
            fetches[state["started"]]().start()
            state["started"] += 1

    def wait_to(n):
        while state["arrived"] < n:
            fetches[state["arrived"]]().wait()
            state["arrived"] += 1
            start_to(state["arrived"] + WINDOW)

    small[0].start()
    start_to(WINDOW)
    for copy in small[1:]:
        copy.start()

    barrier = pltpu.get_barrier_semaphore()

    @pl.loop(1, devices)
    def _(i):
        to = lax.rem(me + i, devices)
        pl.semaphore_signal(
            barrier, inc=1, device_id=(to // cols, lax.rem(to, cols)), device_id_type=MESH
        )

    small[0].wait()
    for d in range(devices):
        line, at = divmod(d * sites, 128)
        piece = flat[line : line + 1, at : min(at + sites, 128)]
        if at + sites > 128:
            piece = jnp.concatenate([piece, flat[line + 1 : line + 2, : at + sites - 128]], axis=1)
        owner[d : d + 1, :] = piece
    own = owner[pl.ds(me, 1), :]
    onehot = lax.broadcasted_iota(jnp.int32, (devices, sites), 0) == own
    onehot = onehot.astype(jnp.float32)
    before = jnp.dot(
        onehot.astype(jnp.bfloat16), earlier_mask(sites), preferred_element_type=jnp.float32
    )
    rank = jnp.sum(onehot * before, axis=0, keepdims=True).astype(jnp.int32)
    slot = lax.broadcasted_iota(jnp.int32, (devices * SLOT, sites), 0)
    placing[...] = (slot == own * SLOT + rank).astype(jnp.float32).astype(jnp.bfloat16)
    for copy in small[1:]:
        copy.wait()

    def send_side(g):
        return pltpu.make_async_remote_copy(
            src_ref=ysend.at[g], dst_ref=yrecv.at[g], send_sem=yssem.at[g], recv_sem=yrsem.at[g],
            device_id=(row, col + 1 - 2 * side), device_id_type=MESH,
        )

    def send_group(g):
        return pltpu.make_async_remote_copy(
            src_ref=zsend.at[g], dst_ref=zrecv.at[g], send_sem=zssem.at[g], recv_sem=zrsem.at[g],
            device_id=(row, group_at(g) * 2 + side), device_id_type=MESH,
        )

    lag = 2 if PAIRED else 4
    pending = []
    first = 0
    for n, step in enumerate(steps):
        count = len(step)
        lo, hi = first * sites, (first + count) * sites
        if n == 0:
            acc = jnp.zeros((count * sites, events), jnp.float32)
            for j in range(chunks):
                wait_to(count + j + 1)
                acc += jnp.dot(
                    fbuf[lo:hi, j * cut : (j + 1) * cut], dbuf[j * cut : (j + 1) * cut, :],
                    preferred_element_type=jnp.float32,
                )
            pl.semaphore_wait(barrier, devices - 1)
        else:
            wait_to(chunks + first + count)
            acc = jnp.dot(fbuf[lo:hi, :], dbuf[...], preferred_element_type=jnp.float32)
        for b, (kind, g) in enumerate(step):
            part = acc[b * sites : (b + 1) * sites]
            if kind == "A":
                ysend[g] = part.astype(jnp.bfloat16)
                send_side(g).start()
            else:
                held[g] = part
                if g < groups - 1:
                    pending.append(g)
        last = n == len(steps) - 1
        while pending and (last or n >= sent_at["A", pending[0]] + lag):
            g = pending.pop(0)
            send_side(g).wait_recv()
            zsend[g] = (held[g] + yrecv[g].astype(jnp.float32)).astype(jnp.bfloat16)
            send_group(g).start()
        first += count

    own_group = groups - 1
    send_side(own_group).wait_recv()
    total = held[own_group] + yrecv[own_group].astype(jnp.float32)
    for g in range(groups - 1):
        send_group(g).wait_recv()
        total = total + zrecv[g].astype(jnp.float32)
    res_ref[...] = total
    written = [pltpu.make_async_copy(res_ref, res_out, outsem.at[0])]
    written[0].start()
    motion = (median_log + intra_scale * total + inter[...]).astype(jnp.bfloat16)
    parts = [
        jnp.dot(placing[...], motion[:, h * half : (h + 1) * half], preferred_element_type=jnp.float32)
        .reshape(devices, SLOT, half)
        for h in range(2)
    ]
    outbuf[...] = jnp.concatenate(parts, axis=1).astype(jnp.bfloat16)

    @pl.loop(0, devices)
    def _(i):
        to_group = lax.rem(group + groups // 2 + i // (2 * rows), groups)
        to_row = lax.rem(row + (i // 2) % rows, rows)
        to_col = to_group * 2 + lax.rem(side + i, 2)
        to = to_row * cols + to_col

        @pl.when(to != me)
        def _():
            pltpu.make_async_remote_copy(
                src_ref=outbuf.at[to], dst_ref=inbuf.at[me], send_sem=ssem, recv_sem=rsem,
                device_id=(to_row, to_col), device_id_type=MESH,
            ).start()

    inbuf[me] = outbuf[me]
    prepare_assets(
        me, count_ref[0], owner, site_ref, class_ref, value_ref, curve_ref,
        select_ref, table_ref, agg_ref,
    )
    for g in range(groups):
        send_side(g).wait_send()
    for g in range(groups - 1):
        send_group(g).wait_send()
    others = pl.ds(0, devices - 1)
    pltpu.make_async_copy(inbuf.at[others], inbuf.at[others], rsem).wait()
    levels = curve_ref.shape[0]
    came = inbuf[...].astype(jnp.float32)
    for h in range(2):
        felt = came[:, h * SLOT : (h + 1) * SLOT, :].reshape(devices * SLOT, half)
        level = jnp.clip((felt - grid_low) * ((levels - 1) / grid_span), 0.0, levels - 1.0)
        below = jnp.minimum(level.astype(jnp.int32), levels - 2)
        floor = below.astype(jnp.float32)
        share = level - floor
        stage_ref[:, h * half : (h + 1) * half] = floor.astype(jnp.bfloat16)
        stage_ref[:, events + h * half : events + (h + 1) * half] = share.astype(jnp.bfloat16)
        loss = curve_at(agg_ref[...], below, share)
        regions[0, :, h * half : (h + 1) * half] = jnp.sum(loss.reshape(devices, 8, half), axis=0)
    copies = []
    for i in range(1, rows):
        copy = pltpu.make_async_remote_copy(
            src_ref=regions.at[0], dst_ref=regions.at[i], send_sem=gssem.at[i], recv_sem=grsem.at[i],
            device_id=(lax.rem(row + i, rows), col), device_id_type=MESH,
        )
        copy.start()
        copies.append(copy)
    assets = loss_ref.shape[0]
    for base in range(0, assets, TILE):
        at = slice(base, base + TILE)
        loss_ref[at, :] = tile_losses(select_ref[:, at], table_ref[at, :], stage_ref[...])
        part = pl.ds(base, TILE)
        copy = pltpu.make_async_copy(loss_ref.at[part], loss_out.at[part], outsem.at[2 + base // TILE])
        copy.start()
        written.append(copy)
    pltpu.make_async_copy(outbuf.at[others], outbuf.at[others], ssem).wait()
    total = regions[0]
    for i, copy in enumerate(copies):
        copy.wait_recv()
        total = total + regions[i + 1]
    scale = 1.0 / (assets * rows)
    region_ref[...] = jnp.sum(total, axis=0, keepdims=True) * scale
    copy = pltpu.make_async_copy(region_ref, region_out, outsem.at[1])
    copy.start()
    written.append(copy)
    for copy in copies:
        copy.wait_send()
    for copy in written:
        copy.wait()


def curve_at(table, below, share):
    low = jnp.take_along_axis(table[:, :128], below, axis=1, mode="promise_in_bounds")
    rise = jnp.take_along_axis(table[:, 128:], below, axis=1, mode="promise_in_bounds")
    return low + share * rise


def tile_losses(select, table, stage):
    felt = lax.dot_general(select, stage, (((0,), (0,)), ((), ())), preferred_element_type=jnp.float32)
    events = stage.shape[1] // 2
    parts = []
    for h in range(events // 128):
        below = felt[:, h * 128 : (h + 1) * 128].astype(jnp.int32)
        share = felt[:, events + h * 128 : events + (h + 1) * 128]
        parts.append(curve_at(table, below, share))
    return jnp.concatenate(parts, axis=1)


def prepare_assets(
    me, count, owner, site_ref, class_ref, value_ref, curve_ref, select_ref, table_ref, agg_ref,
):
    devices, sites = owner.shape
    slots = select_ref.shape[0]
    assets = site_ref.shape[1]
    levels, classes = curve_ref.shape
    wide = jnp.broadcast_to(owner[...][:, None, :], (devices, SLOT, sites)).reshape(slots, sites)
    mine = (wide == me).astype(jnp.float32)
    rank = jnp.dot(mine.astype(jnp.bfloat16), earlier_mask(sites), preferred_element_type=jnp.float32)
    slot = lax.broadcasted_iota(jnp.int32, (slots, sites), 0)
    wanted = lax.rem(slot, SLOT).astype(jnp.float32)
    number = (slot // SLOT) * sites + lax.broadcasted_iota(jnp.int32, (slots, sites), 1) + 1
    hit = jnp.where((mine > 0.0) & (rank == wanted), number, 0)
    mysite = jnp.sum(hit, axis=1, keepdims=True) - 1
    curve = curve_ref[...].astype(jnp.float32)
    blank = jnp.zeros((128 - levels, classes), jnp.float32)
    curve = jnp.concatenate([curve, blank, curve[1:], curve[levels - 1 :], blank], axis=0)
    curve = curve.astype(jnp.bfloat16)
    value = value_ref[...].astype(jnp.float32)
    agg = jnp.zeros((slots, 256), jnp.float32)
    for base in range(0, assets, TILE):
        at = slice(base, base + TILE)
        select = (mysite == site_ref[:, at]).astype(jnp.float32)
        owned = jnp.sum(select, axis=0, keepdims=True)
        select = select.astype(jnp.bfloat16)
        select_ref[:, at] = select
        place = base + lax.broadcasted_iota(jnp.int32, (1, TILE), 1)
        live = jnp.where(place < count, owned, 0.0)
        first = base // 128
        price = jnp.concatenate([value[first + i : first + i + 1] for i in range(TILE // 128)], axis=1)
        chosen = lax.broadcasted_iota(jnp.int32, (classes, TILE), 0) == class_ref[:, at]
        chosen = jnp.where(chosen, price * live, 0.0).astype(jnp.bfloat16)
        table = lax.dot_general(
            chosen, curve, (((0,), (1,)), ((), ())), preferred_element_type=jnp.float32
        )
        table = jnp.concatenate([table[:, :128], table[:, 128:] - table[:, :128]], axis=1)
        table_ref[at, :] = table
        agg = agg + jnp.dot(select, table.astype(jnp.bfloat16), preferred_element_type=jnp.float32)
    agg_ref[...] = agg


def write_kernel(parts, res_in, loss_in, region_in, res_out, loss_out, region_out, res, loss, region, came, sent):
    cut = loss.shape[0] // parts
    moves = [(res_in, res, res_out), (region_in, region, region_out)]
    for i in range(parts):
        part = pl.ds(i * cut, cut)
        moves.append((loss_in.at[part], loss.at[part], loss_out.at[part]))
    reads = [pltpu.make_async_copy(src, mid, came.at[i]) for i, (src, mid, _) in enumerate(moves)]
    writes = [pltpu.make_async_copy(mid, dst, sent.at[i]) for i, (_, mid, dst) in enumerate(moves)]
    for read in reads[::-1]:
        read.start()
    for read, write in zip(reads[::-1], writes[::-1]):
        read.wait()
        write.start()
    for write in writes:
        write.wait()


def body(
    rows, cols,
    factor_panel, normal_draws, inter_event, site_owner, asset_site, asset_class, asset_value, asset_count, damage_curve,
):
    devices = rows * cols
    groups = cols // 2
    local, depth = factor_panel.shape
    sites = local // cols
    events = normal_draws.shape[1]
    assets = asset_site.shape[0]
    slots = devices * SLOT
    chunks = 3
    hbm = pl.BlockSpec(memory_space=pltpu.HBM)
    dma = pltpu.SemaphoreType.DMA
    bf16, f32, i32 = jnp.bfloat16, jnp.float32, jnp.int32
    shapes = (
        jax.ShapeDtypeStruct((sites, events), f32),
        jax.ShapeDtypeStruct((assets, events), f32),
        jax.ShapeDtypeStruct((1, events), f32),
    )
    res, loss, region = pl.pallas_call(
        functools.partial(motion_kernel, rows, cols),
        out_shape=shapes,
        in_specs=[hbm] * 9,
        out_specs=(hbm,) * 3,
        scratch_shapes=[
            pltpu.VMEM((sites, events), f32),
            pltpu.VMEM((assets, events), f32),
            pltpu.VMEM((1, events), f32),
            pltpu.VMEM((slots, assets), bf16),
            pltpu.VMEM((assets, 256), f32),
            pltpu.VMEM((slots, 2 * events), bf16),
            pltpu.VMEM((local, depth), bf16),
            pltpu.VMEM((depth, events), bf16),
            pltpu.VMEM((groups, sites, events), bf16),
            pltpu.VMEM((groups, sites, events), bf16),
            pltpu.VMEM((groups, sites, events), f32),
            pltpu.VMEM((groups, sites, events), bf16),
            pltpu.VMEM((groups, sites, events), bf16),
            pltpu.VMEM((slots, sites), bf16),
            pltpu.VMEM((devices, 2 * SLOT, events // 2), bf16),
            pltpu.VMEM((devices, 2 * SLOT, events // 2), bf16),
            pltpu.VMEM((rows, 8, events), f32),
            pltpu.VMEM((slots, 256), f32),
            pltpu.VMEM((devices, sites), i32),
            pltpu.SMEM((1,), i32),
            pltpu.VMEM((1, events), f32),
            pltpu.VMEM((devices * sites // 128, 128), i32),
            pltpu.VMEM((1, assets), i32),
            pltpu.VMEM((1, assets), i32),
            pltpu.VMEM((assets // 128, 128), bf16),
            pltpu.VMEM(damage_curve.shape, bf16),
            dma((cols,)), dma((chunks,)), dma((groups,)), dma((groups,)), dma((groups,)), dma((groups,)),
            dma, dma, dma((rows,)), dma((rows,)), dma((7,)), dma((2 + assets // TILE,)),
        ],
        compiler_params=pltpu.CompilerParams(
            collective_id=0, has_side_effects=True, vmem_limit_bytes=K1 << 10
        ),
        name="everything",
    )(
        asset_count, factor_panel, normal_draws, inter_event.reshape(1, events), site_owner.reshape(devices * sites // 128, 128),
        asset_site.reshape(1, assets), asset_class.reshape(1, assets),
        asset_value.reshape(assets // 128, 128), damage_curve,
    )
    return pl.pallas_call(
        functools.partial(write_kernel, PARTS),
        out_shape=shapes,
        in_specs=[hbm] * 3,
        out_specs=(hbm,) * 3,
        scratch_shapes=[pltpu.VMEM(shape.shape, f32) for shape in shapes] + [dma((PARTS + 2,)), dma((PARTS + 2,))],
        compiler_params=pltpu.CompilerParams(vmem_limit_bytes=K2 << 20),
        name="writing",
    )(res, loss, region)


def solution(mesh):
    placed = (
        P("row", "col"),
        P("col", None),
        P(),
        P(),
        P(("row", "col")),
        P(("row", "col")),
        P(("row", "col")),
        P(("row", "col")),
        P(),
    )
    return jax.shard_map(
        functools.partial(body, mesh.shape["row"], mesh.shape["col"]),
        mesh=mesh,
        in_specs=placed,
        out_specs=(P(("row", "col"), None), P(("row", "col"), None), P("col", None)),
        check_vma=False,
    )
```

time: 44.3 us -> 37.7 us (0.85)
  local copies, waits for them, and re-layouts: 6.77 us -> 0 us
    unnamed x13 -> x0, local copies, waits for them, and re-layouts: 5.98 us -> none
    reshape x1 -> x0, local copies, waits for them, and re-layouts: 0.79 us -> none  [body(): owner = site_owner.reshape(devices, sites)]
    pallas_call x1 -> x2, Pallas kernels: 35.8 us -> 36.1 us  [the longest x1 33.7 us: body(): pl.pallas_call(functools.partial(motion_kernel, rows, cols), out_shape=sh...]
where the time goes in v1:
time: 37.7 us; the launch traced here: 37.4 us
  Pallas kernels  36.1 us (96%)
  between operations  1.29 us (3%)
    pallas_call x1, Pallas kernels, body(): pl.pallas_call(functools.partial(motion_kernel, rows, cols), out_shape=sh...  33.7 us
    pallas_call x1, Pallas kernels, body(): pl.pallas_call(functools.partial(write_kernel, PARTS), out_shape=shapes,...  2.48 us

profile of v1, /device:TPU:0, one launch (start us, length us, event | category | flops | bytes accessed | tf_op | source)
XLA Modules:
  0.0 37.4 jit_solution(13077822586446881026)
XLA Ops:
  1.3 33.7 %everything.1 = (f32[112,256]{1,0:T(8,128)}, f32[2048,256]{1,0:T(8,128)}, f32[1,256]{1,0:T(1,128)}) custom-call(s32[1]{0:T(128)S(6)} %copy.12.count_hbm, bf16[896,12288]{1,0:T(8,128)(2,1)} %factor.1, bf16[12288,256]{1,0:T(8,128)(2,1)} %draws.1, f32[1,256]{1,0:T(1,128)} %bitcast.9, s32[28,128]{1,0:T(8,128)} %bitcast.5, s32[1,2048]{1,0:T(1,128)} %bitcast.6, ...), custom_call_target="tpu_custom_call" | custom-call | tf_op jit(solution)/shard_map/everything/pallas_call | solution.py:366
  34.9 2.5 %writing.1 = (f32[112,256]{1,0:T(8,128)}, f32[2048,256]{1,0:T(8,128)}, f32[1,256]{1,0:T(1,128)}) custom-call(f32[112,256]{1,0:T(8,128)} %get-tuple-element.6.res_in, f32[2048,256]{1,0:T(8,128)} %get-tuple-element.7.loss_in, f32[1,256]{1,0:T(1,128)} %get-tuple-element.8.region_in), custom_call_target="tpu_custom_call" | custom-call | tf_op jit(solution)/shard_map/writing/pallas_call | solution.py:410

commit v2 on v1

--- a/solution.py
+++ b/solution.py
@@ -16,7 +16,7 @@
 K1 = 60 * 1024
 K2 = 60
 PARTS = 8
-WINDOW = 4
+WINDOW = 16
 PAIRED = True
 MESH = pl.DeviceIdType.MESH
 
@@ -92,7 +92,7 @@
 
     def start_to(n):
         while state["started"] < min(n, len(fetches)):
-            fetches[state["started"]]().start()
+            fetches[state["started"]]().start(priority=int(state["started"] >= width + chunks))
             state["started"] += 1
 
     def wait_to(n):
@@ -198,19 +198,13 @@
     ]
     outbuf[...] = jnp.concatenate(parts, axis=1).astype(jnp.bfloat16)
 
-    @pl.loop(0, devices)
+    @pl.loop(1, devices)
     def _(i):
-        to_group = lax.rem(group + groups // 2 + i // (2 * rows), groups)
-        to_row = lax.rem(row + (i // 2) % rows, rows)
-        to_col = to_group * 2 + lax.rem(side + i, 2)
-        to = to_row * cols + to_col
-
-        @pl.when(to != me)
-        def _():
-            pltpu.make_async_remote_copy(
-                src_ref=outbuf.at[to], dst_ref=inbuf.at[me], send_sem=ssem, recv_sem=rsem,
-                device_id=(to_row, to_col), device_id_type=MESH,
-            ).start()
+        to = lax.rem(me + i, devices)
+        pltpu.make_async_remote_copy(
+            src_ref=outbuf.at[to], dst_ref=inbuf.at[me], send_sem=ssem, recv_sem=rsem,
+            device_id=(to // cols, lax.rem(to, cols)), device_id_type=MESH,
+        ).start()
 
     inbuf[me] = outbuf[me]
     prepare_assets(

time: 37.7 us -> 36.6 us (0.971)
  Pallas kernels: 36.1 us -> 35.2 us
    pallas_call x1, Pallas kernels: 33.7 us -> 32.7 us  [body(): pl.pallas_call(functools.partial(motion_kernel, rows, cols), out_shape=sh...]
where the time goes in v2:
time: 36.6 us; the launch traced here: 36.5 us
  Pallas kernels  35.2 us (96%)
  between operations  1.29 us (4%)
    pallas_call x1, Pallas kernels, body(): pl.pallas_call(functools.partial(motion_kernel, rows, cols), out_shape=sh...  32.7 us
    pallas_call x1, Pallas kernels, body(): pl.pallas_call(functools.partial(write_kernel, PARTS), out_shape=shapes,...  2.48 us

profile of v2, /device:TPU:0, one launch (start us, length us, event | category | flops | bytes accessed | tf_op | source)
XLA Modules:
  0.0 36.5 jit_solution(14054372142432299950)
XLA Ops:
  1.3 32.7 %everything.1 = (f32[112,256]{1,0:T(8,128)}, f32[2048,256]{1,0:T(8,128)}, f32[1,256]{1,0:T(1,128)}) custom-call(s32[1]{0:T(128)S(6)} %copy.12.count_hbm, bf16[896,12288]{1,0:T(8,128)(2,1)} %factor.1, bf16[12288,256]{1,0:T(8,128)(2,1)} %draws.1, f32[1,256]{1,0:T(1,128)} %bitcast.9, s32[28,128]{1,0:T(8,128)} %bitcast.5, s32[1,2048]{1,0:T(1,128)} %bitcast.6, ...), custom_call_target="tpu_custom_call" | custom-call | tf_op jit(solution)/shard_map/everything/pallas_call | solution.py:360
  34.0 2.5 %writing.1 = (f32[112,256]{1,0:T(8,128)}, f32[2048,256]{1,0:T(8,128)}, f32[1,256]{1,0:T(1,128)}) custom-call(f32[112,256]{1,0:T(8,128)} %get-tuple-element.6.res_in, f32[2048,256]{1,0:T(8,128)} %get-tuple-element.7.loss_in, f32[1,256]{1,0:T(1,128)} %get-tuple-element.8.region_in), custom_call_target="tpu_custom_call" | custom-call | tf_op jit(solution)/shard_map/writing/pallas_call | solution.py:404
